TPU v7x, 32 devices: a whole 2x2x4 slice. The times are simulated.
32 devices in a mesh: sim: 2 (over y), band: 4 (over z), ord: 4 (over x, core).
Axes of the slice: x: 2, y: 2, z: 4, core: 2. Of those that a mesh axis runs over, the one named last changes fastest.
Arguments:
- alm: bfloat16 [12, 256, 8192], P('sim', 'ord', 'band'), parts along dimension 0, may hold values from -6 to 6
- legendre: bfloat16 [16, 256, 8192], P(None, 'ord', 'band'), may hold values from -0.005859375 to 0.005859375
- order_ids: int32 [256], P('ord'), may hold values from 0 to 8191, as said below
- cycle_number: int32 [16], P('band'), may hold values from 1 to 32767
- src_band: int32 [4096, 1], P(('sim', 'band', 'ord')), parts along dimension 0, may hold values from 0 to 3; in each aligned block of 128 rows (0 to 127, 128 to 255, ...) at most 64 rows name the same one
- src_block: int32 [4096], P(('sim', 'band', 'ord')), parts along dimension 0, may hold values from 0 to 127
- weights: bfloat16 [4096, 128, 128], P(('sim', 'band', 'ord')), parts along dimension 0, may hold values from -0.5 to 0.5
Outputs:
- sky_map: bfloat16 [6, 16, 16384], P('sim', 'band', 'ord'), parts along dimension 0
- lensed: float32 [6, 16, 16384], P('sim', 'band', 'ord'), parts along dimension 0
There are 2 independent parts, one for each index of `sim`. A program takes and returns all parts, laid end to end along the dimension named above; an argument that names none is the same for every part. Nothing has to cross between parts.
Inputs may be any that keep to these rules, and one draw needn't show every extreme that they name: `src_band`: among the blocks of one device at most 64 name the same band, a bound that some block reaches. `order_ids`: distinct values; one of them is 0.
All inputs are finite; a program needn't handle non-finite values.
Results may differ from a plain program's by a relative error of at most 0.0029.
Values may be sent and summed in bfloat16 or wider, within the bound.
A program may use at most 128 MiB of HBM per device.

v0:
```python
import math

import jax
import jax.numpy as jnp
from jax import lax
from jax.sharding import PartitionSpec as P

NPIX = 16384
BLK = 128


def rotate(coeffs, order_ids, cycle_number):
    parity = (cycle_number % 2).astype(jnp.float32)
    orders = order_ids.astype(jnp.float32)
    angle = math.pi / NPIX * orders[None, :] * parity[:, None]
    cosine = jnp.cos(angle)[:, None, :]
    sine = jnp.sin(angle)[:, None, :]
    factor = jnp.where(order_ids == 0, 1.0, 2.0).astype(jnp.float32)[None, None, :]
    real_part = coeffs[:, 0:3, :]
    imag_part = coeffs[:, 3:6, :]
    rot_re = factor * (real_part * cosine - imag_part * sine)
    rot_im = factor * (real_part * sine + imag_part * cosine)
    return (rot_re, rot_im)


def synthesize(rot_re, rot_im, order_ids, columns):
    phase = order_ids[:, None] * columns[None, :] % NPIX
    angle = phase.astype(jnp.float32) * (2.0 * math.pi / NPIX)
    right = jnp.concatenate([jnp.cos(angle), jnp.sin(angle)], axis=0)
    cycles = rot_re.shape[0]
    left = jnp.concatenate([rot_re, -rot_im], axis=2).reshape(cycles * 3, -1)
    pixels = jnp.dot(
        left, right, precision=lax.Precision.HIGHEST, preferred_element_type=jnp.float32
    )
    return jnp.transpose(pixels.reshape(cycles, 3, -1), (1, 0, 2))


def local(alm, legendre, order_ids, cycle_number, src_band, src_block, weights):
    cycles_here = cycle_number.shape[0]
    orders_here = order_ids.shape[0]
    npix_here = NPIX // lax.axis_size("ord")
    part = jnp.einsum("rml,cml->rcm", legendre, alm, preferred_element_type=jnp.float32)
    coeffs = lax.psum_scatter(
        part.reshape(cycles_here * lax.axis_size("band"), 6 * orders_here),
        "band",
        scatter_dimension=0,
        tiled=True,
    )
    coeffs = coeffs.reshape(cycles_here, 6, orders_here)
    all_coeffs, all_orders = (
        lax.all_gather(coeffs, "ord", axis=2, tiled=True),
        lax.all_gather(order_ids, "ord", axis=0, tiled=True),
    )
    rot_re, rot_im = rotate(all_coeffs, all_orders, cycle_number)
    columns = lax.axis_index("ord") * npix_here + jnp.arange(npix_here, dtype=jnp.int32)
    sky_map = synthesize(rot_re, rot_im, all_orders, columns).astype(jnp.bfloat16)
    blocks = sky_map.reshape(3, -1, BLK)
    count_blocks = blocks.shape[1]
    bands = lax.axis_size("band")
    capacity = max(2, 2 * count_blocks // bands)
    target = src_band[:, 0]
    onehot = (target[:, None] == jnp.arange(bands, dtype=jnp.int32)[None, :]).astype(jnp.int32)
    before = jnp.cumsum(onehot, axis=0) - onehot
    position = jnp.sum(before * onehot, axis=1)
    slot_index = target * capacity + position
    requests = jnp.full((bands * capacity,), -1, jnp.int32).at[slot_index].set(src_block)
    requests = requests.reshape(bands, capacity)
    picked = blocks[
        :,
        jnp.clip(
            lax.all_to_all(requests, "band", split_axis=0, concat_axis=0, tiled=True),
            0,
            count_blocks - 1,
        ),
        :,
    ]
    received = lax.all_to_all(picked, "band", split_axis=1, concat_axis=1, tiled=True)
    source = received.reshape(3, bands * capacity, BLK)[:, slot_index, :]
    lensed = jnp.einsum("kij,ckj->cki", weights, source, preferred_element_type=jnp.float32)
    return (sky_map, lensed.reshape(3, cycles_here, npix_here))


def solution(mesh):
    placed = (
        P("sim", "ord", "band"),
        P(None, "ord", "band"),
        P("ord"),
        P("band"),
        P(("sim", "band", "ord"), None),
        P(("sim", "band", "ord")),
        P(("sim", "band", "ord"), None, None),
    )
    return jax.shard_map(
        local,
        mesh=mesh,
        in_specs=placed,
        out_specs=(P("sim", "band", "ord"), P("sim", "band", "ord")),
        check_vma=False,
    )
```

profile of v0, /device:TPU:0, one launch (start us, length us, event | category | flops | bytes accessed | tf_op | source)
XLA Modules:
  0.0 94.6 jit_solution(5537024923657637827)
XLA Ops:
  0.6 0.7 fusion.19
  1.4 0.2 reduce_window_sum.11
  1.5 0.8 select_reduce_fusion
  2.4 0.7 fusion.25
  3.0 1.1 %scatter_custom_fusion = s32[256]{0:T(256)S(1)} fusion(s32[128]{0:T(128)S(1)} %fusion.25, s32[128]{0:T(128)} %param.12, s32[]{:T(128)} %constant.56.clone.1), kind=kCustom, calls=%fused_computation.52 | custom fusion | bytes 1536 | tf_op jit(solution)/shard_map/scatter | solution.py:66
  4.2 0.7 all_to_all.9
  4.8 6.3 %all-to-all-start = ((s32[4,1,64]{2,1,0:T(1,128)}), s32[4,1,64]{2,1,0:T(1,128)S(1)}, u32[]{:S(2)}, u32[]{:S(2)}) async-start(s32[4,1,64]{2,1,0:T(1,128)} %all_to_all.9), calls=%async_computation | async-start | bytes 4096 | tf_op jit(solution)/shard_map/all_to_all | solution.py:71
  11.1 1.2 %dynamic-slice = u32[1]{0:T(128)} dynamic-slice(u32[32]{0:T(128)} %constant.63, u32[]{:T(128)S(6)} %add.58), dynamic_slice_sizes={1} | dynamic-slice | bytes 12
  13.0 0.9 dynamic-update-slice
  13.9 4.9 %all-reduce = s32[256]{0:T(256)S(1)} all-reduce(s32[256]{0:T(256)S(1)} %dynamic-update-slice), channel_id=1, replica_groups=mesh['sim'=2,'band'=4,'ord'=4] {'ord'}, use_global_device_ids=true, to_apply=%add | all-reduce | flops 256 | bytes 2048
  18.8 0.7 fusion.23
  19.5 5.8 %fusion.13 = f32[16,6,64]{0,1,2:T(8,128)S(1)} fusion(bf16[16,64,2048]{2,1,0:T(8,128)(2,1)} %param.8, bf16[6,64,2048]{2,1,0:T(8,128)(2,1)} %param.7), kind=kOutput, calls=%fused_computation.23 | convolution fusion | flops 25165824 | bytes 5791744 | tf_op jit(solution)/shard_map/rml,cml->rcm/dot_general | solution.py:42
  25.2 0.1 copy.19
  25.5 19.4 %all-reduce.1 = f32[16,384]{1,0:T(8,128)S(1)} all-reduce(f32[16,384]{1,0:T(8,128)S(1)} %reshape.100), channel_id=2, replica_groups=mesh['sim'=2,'band'=4,'ord'=4] {'band'}, use_global_device_ids=true, to_apply=%region_0.0.clone | all-reduce | flops 6144 | bytes 49152
  44.9 0.6 dynamic-slice.1
  46.2 0.1 copy.20
  46.4 6.7 %all_gather.7 = f32[4,6,256]{1,0,2:T(4,128)S(1)} all-gather(f32[4,6,64]{1,0,2:T(4,128)S(1)} %copy.20), channel_id=1, replica_groups=mesh['sim'=2,'band'=4,'ord'=4] {'ord'}, dimensions={2}, use_global_device_ids=true | all-gather | bytes 30720 | tf_op jit(solution)/shard_map/all_gather | solution.py:51
  53.1 0.3 fusion.29
  53.4 0.2 copy.27
  53.6 0.2 copy.28
  53.9 16.6 %fusion.12 = (f32[256,4096]{1,0:T(8,128)S(1)}, f32[256,4096]{1,0:T(8,128)S(1)}) fusion(s32[4096]{0:T(1024)S(1)} %iota_add_fusion, s32[256]{0:T(256)S(1)} %all-reduce), kind=kLoop, calls=%fused_computation.21 | loop fusion | flops 14680064 | bytes 8406016 | tf_op jit(solution)/shard_map/cos | solution.py:29
  70.5 0.1 multiply_cosine_fusion
  70.6 4.2 %fusion.4 = bf16[3,4,4096]{2,1,0:T(4,128)(2,1)S(1)} fusion(f32[256,4096]{1,0:T(8,128)S(1)} %get-tuple-element.7, f32[256,4096]{1,0:T(8,128)S(1)} %get-tuple-element.6, f32[4,3,256]{2,0,1:T(4,128)S(1)} %get-tuple-element.5, f32[4,3,256]{2,0,1:T(4,128)S(1)} %get-tuple-element.4), kind=kOutput, calls=%fused_computation.13 | convolution fusion | flops 304142336 | bytes 8511488 | tf_op jit(solution)/shard_map/dot_general | solution.py:32
  74.8 0.1 reshape.102
  75.1 1.0 %gather_fusion = bf16[256,3,128]{2,1,0:T(4,128)(2,1)S(1)} fusion(bf16[3,128,128]{2,0,1:T(4,128)(2,1)S(1)} %copy.23, s32[1024]{0:T(1024)S(1)} %pad_clamp_fusion.1), kind=kCustom, calls=%fused_computation | custom fusion | bytes 394240 | tf_op jit(solution)/shard_map/gather | solution.py:68
  76.1 0.7 copy.38
  76.8 3.4 %all-to-all-start.1 = ((bf16[3,4,64,128]{3,2,0,1:T(8,128)(2,1)}), bf16[3,4,64,128]{3,2,0,1:T(8,128)(2,1)S(1)}, u32[]{:S(2)}, u32[]{:S(2)}) async-start(bf16[3,4,64,128]{3,2,0,1:T(8,128)(2,1)} %bitcast.33), calls=%async_computation.1 | async-start | bytes 393216 | tf_op jit(solution)/shard_map/all_to_all | solution.py:77
  80.2 8.2 %all-to-all-done.1 = bf16[3,4,64,128]{3,2,0,1:T(8,128)(2,1)S(1)} async-done(((bf16[3,4,64,128]{3,2,0,1:T(8,128)(2,1)}), bf16[3,4,64,128]{3,2,0,1:T(8,128)(2,1)S(1)}, u32[]{:S(2)}, u32[]{:S(2)}) %all-to-all-start.1) | async-done | bytes 196640 | tf_op jit(solution)/shard_map/all_to_all | solution.py:77
  88.4 0.2 copy.25
  88.6 0.7 gather_fusion.1
  89.4 4.4 %convolution_bitcast_fusion = f32[3,128,128]{2,0,1:T(4,128)S(1)} fusion(bf16[128,128,128]{2,1,0:T(8,128)(2,1)} %param.13, bf16[128,3,128]{2,1,0:T(4,128)(2,1)S(1)} %gather_fusion.1), kind=kOutput, calls=%fused_computation.22 | convolution fusion | flops 12582912 | bytes 4489216 | tf_op jit(solution)/shard_map/kij,ckj->cki/dot_general | solution.py:79
  93.8 0.7 reshape.104
  (19 shorter events, 0.5 us)
Async XLA Ops:
  4.2 40.7 %copy-start.1 = (u32[32]{0:T(128)S(1)}, u32[32]{0:T(128)}, u32[]{:S(2)}) copy-start(u32[32]{0:T(128)} %constant.69) | copy-start | bytes 388
  4.8 70.2 %all-to-all-start = ((s32[4,1,64]{2,1,0:T(1,128)}), s32[4,1,64]{2,1,0:T(1,128)S(1)}, u32[]{:S(2)}, u32[]{:S(2)}) async-start(s32[4,1,64]{2,1,0:T(1,128)} %all_to_all.9), calls=%async_computation | async-start | bytes 4096 | tf_op jit(solution)/shard_map/all_to_all | solution.py:71
  74.8 19.8 %copy-start = (bf16[3,4,4096]{2,1,0:T(4,128)(2,1)}, bf16[3,4,4096]{2,1,0:T(4,128)(2,1)S(1)}, u32[]{:S(2)}) copy-start(bf16[3,4,4096]{2,1,0:T(4,128)(2,1)S(1)} %fusion.4) | copy-start | bytes 294916
  76.8 11.6 %all-to-all-start.1 = ((bf16[3,4,64,128]{3,2,0,1:T(8,128)(2,1)}), bf16[3,4,64,128]{3,2,0,1:T(8,128)(2,1)S(1)}, u32[]{:S(2)}, u32[]{:S(2)}) async-start(bf16[3,4,64,128]{3,2,0,1:T(8,128)(2,1)} %bitcast.33), calls=%async_computation.1 | async-start | bytes 393216 | tf_op jit(solution)/shard_map/all_to_all | solution.py:77
where the time goes:
time: 95 us; the launch traced here: 94.6 us
  blocking collectives  31.1 us (33%)
  other arithmetic  19.8 us (21%)
  matrix products  14.4 us (15%)
  starting transfers between devices  9.68 us (10%)
  local copies, waits for them, and re-layouts  9.33 us (10%)
  waiting for transfers between devices  8.22 us (9%)
  between operations  2.1 us (2%)
    unnamed x2, blocking collectives  24.3 us
    cos x1, other arithmetic, synthesize(): right = jnp.concatenate([jnp.cos(angle), jnp.sin(angle)], axis=0)  16.6 us
    all_to_all x1, waiting for transfers between devices, local(): lax.all_to_all(picked, 'band', split_axis=1, concat_axis=1, tiled=True)  8.21 us
    all_gather x1, blocking collectives, local(): lax.all_gather(coeffs, 'ord', axis=2, tiled=True)  6.72 us
    all_to_all x1, starting transfers between devices, local(): lax.all_to_all(requests, 'band', split_axis=0, concat_axis=0, tiled=True)  6.32 us
    dot_general x1, matrix products, local(): jnp.einsum('rml,cml->rcm', legendre, alm, preferred_element_type=jnp.floa...  5.76 us
    dot_general x1, matrix products, local(): jnp.einsum('kij,ckj->cki', weights, source, preferred_element_type=jnp.fl...  4.43 us
    dot_general x1, matrix products, synthesize(): jnp.dot(left, right, precision=lax.Precision.HIGHEST, preferred_element_t...  4.16 us
  transfers between devices with their start and end apart: 2, of which 1 were waited for; matrix products, arithmetic and copies ran while one was open for 33% of the time, Pallas kernels for 0%

commit v1 on v0

v1 whole, which is shorter than its diff:
```python
import functools
import math

import jax
import jax.numpy as jnp
from jax import lax
from jax.experimental import pallas as pl
from jax.experimental.pallas import tpu as pltpu
from jax.sharding import PartitionSpec as P

BLK = 128
MESH = pl.DeviceIdType.MESH
SUB = 16
WIDE = 256
CHUNKS = 4


def cosine(phase, period):
    half, quarter = period // 2, period // 4
    centred = ((phase + half) & (period - 1)) - half
    x = (quarter - jnp.abs(centred)).astype(jnp.float32) * (2.0 * math.pi / period)
    y = x * x
    tail = -1.0 / 39916800 * y + 1.0 / 362880
    tail = tail * y - 1.0 / 5040
    tail = tail * y + 1.0 / 120
    tail = tail * y - 1.0 / 6
    return x + x * y * tail


def exchange(bands, ords, cyc, npix, cycle_ref, order_ref, alm_ref, leg_ref, out_ref,
             alm_buf, leg_buf, part, landed, mine, gathered,
             alm_sem, leg_sem, rs_send, rs_recv, ag_send, ag_recv):
    b, o = lax.axis_index("band"), lax.axis_index("ord")
    devices = bands * ords
    me = b * ords + o
    chunks = alm_buf.shape[0]
    cycles = leg_buf.shape[1]
    rows = part.shape[1]
    half = chunks * SUB

    def fetch_alm(q):
        return pltpu.make_async_copy(
            alm_ref.at[:, pl.ds(q * SUB, SUB), :], alm_buf.at[q, pl.ds(0, 6)], alm_sem.at[q])

    def fetch_leg(q):
        return pltpu.make_async_copy(
            leg_ref.at[:, pl.ds(q * SUB, SUB), :], leg_buf.at[q], leg_sem.at[q])

    for q in range(chunks):
        fetch_alm(q).start()
        fetch_leg(q).start()

    barrier = pltpu.get_barrier_semaphore()

    def greet(t, _):
        to = lax.rem(me + t, devices)
        pl.semaphore_signal(barrier, inc=1, device_id={"band": to // ords, "ord": lax.rem(to, ords)},
                            device_id_type=MESH)
        return 0

    lax.fori_loop(1, devices, greet, 0)

    near = lax.broadcasted_iota(jnp.int32, (1, SUB, BLK), 1)
    far = lax.broadcasted_iota(jnp.int32, (1, SUB, BLK), 2) % SUB
    keep = near == far
    lane = lax.broadcasted_iota(jnp.int32, (cycles, BLK), 1)
    packed = [jnp.zeros((cycles, BLK), jnp.float32) for _ in range(3)]
    for q in range(chunks):
        alm_buf[q, 6:8] = jnp.zeros((2, SUB, alm_buf.shape[3]), jnp.bfloat16)
        fetch_alm(q).wait()
        fetch_leg(q).wait()
        depth = alm_buf.shape[3]
        product = lax.dot_general(
            leg_buf[q].reshape(cycles * SUB, depth), alm_buf[q].reshape(8 * SUB, depth),
            (((1,), (1,)), ((), ())), preferred_element_type=jnp.float32)
        diag = jnp.sum(jnp.where(keep, product.reshape(cycles, SUB, BLK), 0.0), axis=1)
        for f in range(3):
            for side in range(2):
                start = side * half + q * SUB
                shift = (start - (f + 3 * side) * SUB) % BLK
                moved = pltpu.roll(diag, shift, 1) if shift else diag
                packed[f] = jnp.where((lane >= start) & (lane < start + SUB), moved, packed[f])
    part[:, 3 * cyc:rows, :] = jnp.zeros((bands, rows - 3 * cyc, BLK), jnp.float32)
    for f in range(3):
        for d in range(bands):
            part[d, f * cyc:(f + 1) * cyc, :] = packed[f][d * cyc:(d + 1) * cyc]

    pl.semaphore_wait(barrier, devices - 1)

    def scatter(t):
        to = lax.rem(b + t, bands)
        return pltpu.make_async_remote_copy(
            src_ref=part.at[to], dst_ref=landed.at[t], send_sem=rs_send.at[t], recv_sem=rs_recv.at[t],
            device_id={"band": to}, device_id_type=MESH)

    def begin(make):
        def step(t, _):
            make(t).start()
            return 0
        return step

    def ended(make):
        def step(t, _):
            make(t).wait()
            return 0
        return step

    lax.fori_loop(1, bands, begin(scatter), 0)

    m = order_ref[...]
    row = lax.broadcasted_iota(jnp.int32, (rows, BLK), 0)
    side = lax.broadcasted_iota(jnp.int32, (rows, BLK), 1) // half
    parity = jnp.zeros((rows, BLK), jnp.int32)
    for r in range(cyc):
        parity = jnp.where(row % cyc == r, cycle_ref[r] & 1, parity)
    angle = m * parity
    cos_a = cosine(angle, 2 * npix)
    sin_a = cosine(angle + jnp.where(side == 0, npix // 2, npix // 2 * 3), 2 * npix)
    factor = jnp.where(m == 0, 1.0, 2.0)

    lax.fori_loop(1, bands, ended(scatter), 0)

    total = lax.fori_loop(1, bands, lambda t, acc: acc + landed[t], part[b])
    turned = factor * (total * cos_a + pltpu.roll(total, half, 1) * sin_a)
    turned = jnp.where(row == 3 * cyc, m.astype(jnp.float32), turned)
    mine[...] = turned

    def spread(t):
        to = lax.rem(me + t, devices)
        return pltpu.make_async_remote_copy(
            src_ref=mine, dst_ref=gathered.at[t], send_sem=ag_send.at[t], recv_sem=ag_recv.at[t],
            device_id={"band": to // ords, "ord": lax.rem(to, ords)}, device_id_type=MESH)

    lax.fori_loop(1, devices, begin(spread), 0)
    out_ref[me] = turned
    lax.fori_loop(1, devices, ended(spread), 0)

    def place(t, _):
        out_ref[lax.rem(me - t + devices, devices)] = gathered[t]
        return 0

    lax.fori_loop(1, devices, place, 0)


def lens(bands, ords, cyc, npix, where_ref, band_ref, block_ref, coef_ref, weights_ref, sky_ref, lensed_ref,
         high, low, table, picked, weights_buf, sem):
    b, o = where_ref[0], where_ref[1]
    here = npix // ords
    groups = here // WIDE
    depth = ords * BLK
    count = weights_buf.shape[0]
    slab = count // CHUNKS
    lines = bands * 3 * cyc
    halves = WIDE // BLK
    per_cycle = here // BLK

    def fetch(c):
        return pltpu.make_async_copy(
            weights_ref.at[pl.ds(c * slab, slab)], weights_buf.at[pl.ds(c * slab, slab)], sem.at[c])

    for c in range(CHUNKS):
        fetch(c).start()

    m = jnp.concatenate([coef_ref[k, 3 * cyc:3 * cyc + 1, :] for k in range(ords)], axis=1).astype(jnp.int32)

    def lanes(count_rows):
        side = (lax.broadcasted_iota(jnp.int32, (count_rows, depth), 1) // (BLK // 2)) % 2
        return lax.broadcasted_iota(jnp.int32, (count_rows, depth), 0), side

    pixel, side = lanes(WIDE)
    waves = cosine(m * pixel + side * (npix // 4), npix)
    waves_high = waves.astype(jnp.bfloat16)
    waves_low = (waves - waves_high.astype(jnp.float32)).astype(jnp.bfloat16)
    group, side = lanes(groups)
    start = m * (o * here + group * WIDE)
    cos_g = cosine(start, npix)
    sin_g = cosine(start + jnp.where(side == 0, npix // 4, npix // 4 * 3), npix)

    for d in range(bands):
        plain = jnp.concatenate([coef_ref[d * ords + k, 0:3 * cyc, :] for k in range(ords)], axis=1)
        swapped = jnp.concatenate(
            [pltpu.roll(coef_ref[d * ords + k], BLK // 2, 1)[0:3 * cyc] for k in range(ords)], axis=1)
        for g in range(groups):
            value = plain * cos_g[g:g + 1] + swapped * sin_g[g:g + 1]
            upper = value.astype(jnp.bfloat16).astype(jnp.float32)
            at = g * lines + d * 3 * cyc
            high[at:at + 3 * cyc, :] = upper
            low[at:at + 3 * cyc, :] = value - upper

    span = min(lines * groups, 768)
    for s in range(0, lines * groups, span):
        left_high = high[s:s + span, :].astype(jnp.bfloat16)
        left_low = low[s:s + span, :].astype(jnp.bfloat16)

        def times(left, right):
            return lax.dot_general(left, right, (((1,), (1,)), ((), ())), preferred_element_type=jnp.float32)

        pixels = times(left_high, waves_high) + (times(left_high, waves_low) + times(left_low, waves_high))
        pixels = pixels.astype(jnp.bfloat16).astype(jnp.float32)
        for h in range(halves):
            table[h, s:s + span, :] = pixels[:, h * BLK:(h + 1) * BLK]

    for g in range(groups):
        for h in range(halves):
            for f in range(3):
                value = table[h, pl.ds(g * lines + b * (3 * cyc) + f * cyc, cyc), :]
                at = g * WIDE + h * BLK
                sky_ref[f, :, at:at + BLK] = value.astype(jnp.bfloat16)

    for c in range(CHUNKS):
        fetch(c).wait()

    def pick(p, _):
        for r in range(cyc):
            n = r * per_cycle + p
            block = block_ref[n]
            cycle, spot = block // per_cycle, block % per_cycle
            line = (spot // halves) * lines + band_ref[n] * (3 * cyc) + cycle
            for f in range(3):
                picked[n, pl.ds(f, 1), :] = table[spot % halves, pl.ds(line + f * cyc, 1), :]
        return 0

    lax.fori_loop(0, per_cycle, pick, 0, unroll=2)

    def apply(p, _):
        for r in range(cyc):
            n = r * per_cycle + p
            made = lax.dot_general(
                picked[n].astype(jnp.bfloat16), weights_buf[n], (((1,), (1,)), ((), ())),
                preferred_element_type=jnp.float32)
            for f in range(3):
                lensed_ref[f, r:r + 1, pl.ds(pl.multiple_of(p * BLK, BLK), BLK)] = made[f:f + 1]
        return 0

    lax.fori_loop(0, per_cycle, apply, 0, unroll=4)


def local(bands, ords, npix, alm, legendre, order_ids, cycle_number, src_band, src_block, weights):
    cyc = cycle_number.shape[0]
    orders = order_ids.shape[0]
    depth = alm.shape[2]
    cycles = legendre.shape[0]
    chunks = orders // SUB
    rows = -(-(3 * cyc + 1) // 8) * 8
    devices = bands * ords
    here = npix // ords
    vmem = pl.BlockSpec(memory_space=pltpu.VMEM)
    smem = pl.BlockSpec(memory_space=pltpu.SMEM)
    anywhere = pl.BlockSpec(memory_space=pl.ANY)
    doubled = jnp.concatenate([order_ids, order_ids]).reshape(1, 2 * orders)
    coef = pl.pallas_call(
        functools.partial(exchange, bands, ords, cyc, npix),
        out_shape=jax.ShapeDtypeStruct((devices, rows, BLK), jnp.float32),
        in_specs=[smem, vmem, anywhere, anywhere],
        out_specs=vmem,
        scratch_shapes=[
            pltpu.VMEM((chunks, 8, SUB, depth), jnp.bfloat16),
            pltpu.VMEM((chunks, cycles, SUB, depth), jnp.bfloat16),
            pltpu.VMEM((bands, rows, BLK), jnp.float32),
            pltpu.VMEM((bands, rows, BLK), jnp.float32),
            pltpu.VMEM((rows, BLK), jnp.float32),
            pltpu.VMEM((devices, rows, BLK), jnp.float32),
            pltpu.SemaphoreType.DMA((chunks,)),
            pltpu.SemaphoreType.DMA((chunks,)),
            pltpu.SemaphoreType.DMA((bands,)),
            pltpu.SemaphoreType.DMA((bands,)),
            pltpu.SemaphoreType.DMA((devices,)),
            pltpu.SemaphoreType.DMA((devices,)),
        ],
        compiler_params=pltpu.CompilerParams(
            collective_id=0, has_side_effects=True, vmem_limit_bytes=24 * 2**20),
        name="exchange",
    )(cycle_number, doubled, alm, legendre)
    place = jnp.stack([lax.axis_index("band"), lax.axis_index("ord")]).astype(jnp.int32)
    lines = bands * 3 * cyc * (here // WIDE)
    count = weights.shape[0]
    return pl.pallas_call(
        functools.partial(lens, bands, ords, cyc, npix),
        out_shape=(
            jax.ShapeDtypeStruct((3, cyc, here), jnp.bfloat16),
            jax.ShapeDtypeStruct((3, cyc, here), jnp.float32),
        ),
        in_specs=[smem, smem, smem, vmem, anywhere],
        out_specs=(vmem, vmem),
        scratch_shapes=[
            pltpu.VMEM((lines, ords * BLK), jnp.float32),
            pltpu.VMEM((lines, ords * BLK), jnp.float32),
            pltpu.VMEM((WIDE // BLK, lines, BLK), jnp.float32),
            pltpu.VMEM((count, 8, BLK), jnp.float32),
            pltpu.VMEM(weights.shape, jnp.bfloat16),
            pltpu.SemaphoreType.DMA((CHUNKS,)),
        ],
        compiler_params=pltpu.CompilerParams(vmem_limit_bytes=48 * 2**20),
        name="lens",
    )(place, src_band.reshape(count), src_block, coef, weights)


def solution(mesh):
    placed = (
        P("sim", "ord", "band"),
        P(None, "ord", "band"),
        P("ord"),
        P("band"),
        P(("sim", "band", "ord"), None),
        P(("sim", "band", "ord")),
        P(("sim", "band", "ord"), None, None),
    )

    def whole(alm, legendre, order_ids, cycle_number, src_band, src_block, weights):
        blocks = weights.shape[0] // mesh.shape["sim"]
        npix = blocks * weights.shape[2] // cycle_number.shape[0]
        return jax.shard_map(
            functools.partial(local, mesh.shape["band"], mesh.shape["ord"], npix),
            mesh=mesh,
            in_specs=placed,
            out_specs=(P("sim", "band", "ord"), P("sim", "band", "ord")),
            check_vma=False,
        )(alm, legendre, order_ids, cycle_number, src_band, src_block, weights)

    return whole
```

time: 95 us -> 30.1 us (0.32)
  blocking collectives: 31.1 us -> 0 us
  Pallas kernels: 0 us -> 23.8 us
  other arithmetic: 19.8 us -> 0.97 us
  matrix products: 14.4 us -> 0 us
  starting transfers between devices: 9.68 us -> 0 us
  waiting for transfers between devices: 8.22 us -> 0 us
  local copies, waits for them, and re-layouts: 9.33 us -> 4.52 us
  between operations: 2.1 us -> 0.69 us
    unnamed x2 -> x0, blocking collectives: 24.3 us -> none
    pallas_call x0 -> x2, Pallas kernels: none -> 23.8 us  [the longest x1 15.7 us: local(): pl.pallas_call(functools.partial(exchange, bands, ords, cyc, npix), out_s...]
    cos x2 -> x0, other arithmetic: 16.7 us -> none  [the longest x1 16.6 us: synthesize(): right = jnp.concatenate([jnp.cos(angle), jnp.sin(angle)], axis=0)]
    dot_general x3 -> x0, matrix products: 14.4 us -> none  [the longest x1 5.76 us: local(): jnp.einsum('rml,cml->rcm', legendre, alm, preferred_element_type=jnp.floa...]
    all_to_all x2 -> x0, starting transfers between devices: 9.68 us -> none  [the longest x1 6.32 us: local(): lax.all_to_all(requests, 'band', split_axis=0, concat_axis=0, tiled=True)]
    all_to_all x2 -> x0, waiting for transfers between devices: 8.22 us -> none  [the longest x1 8.21 us: local(): lax.all_to_all(picked, 'band', split_axis=1, concat_axis=1, tiled=True)]
    all_gather x1 -> x0, blocking collectives: 6.72 us -> none  [local(): lax.all_gather(coeffs, 'ord', axis=2, tiled=True)]
    gather x3 -> x0, local copies, waits for them, and re-layouts: 2.44 us -> none  [the longest x2 1.7 us: local(): blocks[:, jnp.clip(lax.all_to_all(requests, 'band', split_axis=0, concat_...]
  transfers between devices with their start and end apart: 2 -> 0, of which waited for: 1 -> 0; matrix products, arithmetic and copies ran while one was open for 33% -> 0% of each run, Pallas kernels for 0% -> 0%
where the time goes in v1:
time: 30.1 us; the launch traced here: 30 us
  Pallas kernels  23.8 us (79%)
  local copies, waits for them, and re-layouts  4.52 us (15%)
  other arithmetic  0.97 us (3%)
  between operations  0.69 us (2%)
    pallas_call x1, Pallas kernels, local(): pl.pallas_call(functools.partial(exchange, bands, ords, cyc, npix), out_s...  15.7 us
    pallas_call x1, Pallas kernels, local(): pl.pallas_call(functools.partial(lens, bands, ords, cyc, npix), out_shape...  8.09 us
    unnamed x12, local copies, waits for them, and re-layouts  4.52 us
    reshape x1, other arithmetic, local(): doubled = jnp.concatenate([order_ids, order_ids]).reshape(1, 2 * orders)  0.9 us

profile of v1, /device:TPU:0, one launch (start us, length us, event | category | flops | bytes accessed | tf_op | source)
XLA Modules:
  0.0 30.0 jit_solution(9250028703863151485)
XLA Ops:
  0.6 0.0 copy-start.5
  0.6 0.0 copy-start.4
  0.7 0.0 copy-start
  0.7 0.1 pad_add_fusion.where_ref
  0.7 0.9 %add_bitcast_fusion.order_ref = s32[1,128]{1,0:T(1,128)S(1)} fusion(s32[64]{0:T(128)} %param.9), kind=kLoop, calls=%fused_computation.1 | loop fusion | flops 128 | bytes 768 | tf_op jit(solution)/shard_map/reshape | solution.py:250
  1.6 0.0 copy-start.1
  1.6 2.4 %copy-done.1 = bf16[16,64,2048]{2,1,0:T(8,128)(2,1)S(1)} copy-done((bf16[16,64,2048]{2,1,0:T(8,128)(2,1)S(1)}, bf16[16,64,2048]{2,1,0:T(8,128)(2,1)}, u32[]{:S(2)}) %copy-start.1) | copy-done | bytes 4194328
  4.1 0.0 copy-start.2
  4.1 1.4 %copy-done.2 = bf16[6,64,2048]{2,1,0:T(8,128)(2,1)S(1)} copy-done((bf16[6,64,2048]{2,1,0:T(8,128)(2,1)S(1)}, bf16[6,64,2048]{2,1,0:T(8,128)(2,1)}, u32[]{:S(2)}) %copy-start.2) | copy-done | bytes 1572888
  5.5 0.0 copy-start.3
  5.5 0.7 %copy-done.3 = s32[4]{0:T(128)S(1)} copy-done((s32[4]{0:T(128)S(1)}, s32[4]{0:T(128)}, u32[]{:S(2)}) %copy-start.3) | copy-done | bytes 40
  6.1 15.7 %exchange.1.coef_ref = f32[16,16,128]{2,1,0:T(8,128)S(1)} custom-call(s32[4]{0:T(128)S(1)} %copy-done.3, s32[1,128]{1,0:T(1,128)S(1)} %add_bitcast_fusion.order_ref, bf16[6,64,2048]{2,1,0:T(8,128)(2,1)S(1)} %copy-done.2, bf16[16,64,2048]{2,1,0:T(8,128)(2,1)S(1)} %copy-done.1), custom_call_target="tpu_custom_call" | custom-call | tf_op jit(solution)/shard_map/exchange/pallas_call | solution.py:251
  21.8 0.0 copy-done.5
  21.8 0.0 copy-done.4
  21.8 0.0 copy-done
  21.9 8.1 %lens.1 = (bf16[3,4,4096]{2,1,0:T(4,128)(2,1)}, f32[3,4,4096]{2,1,0:T(4,128)}) custom-call(s32[2]{0:T(128)S(1)} %pad_add_fusion.where_ref, s32[128]{0:T(128)S(1)} %bitcast.5, s32[128]{0:T(128)S(1)} %copy-done.5, f32[16,16,128]{2,1,0:T(8,128)S(1)} %exchange.1.coef_ref, bf16[128,128,128]{2,1,0:T(8,128)(2,1)S(1)} %copy-done), custom_call_target="tpu_custom_call" | custom-call | tf_op jit(solution)/shard_map/lens/pallas_call | solution.py:277
Async XLA Ops:
  0.6 21.2 %copy-start.5 = (s32[128]{0:T(128)S(1)}, s32[128]{0:T(128)}, u32[]{:S(2)}) copy-start(s32[128]{0:T(128)} %block_ref.1) | copy-start | bytes 1540
  0.6 21.2 %copy-start.4 = (s32[128,1]{0,1:T(1,128)S(1)}, s32[128,1]{0,1:T(1,128)}, u32[]{:S(2)}) copy-start(s32[128,1]{0,1:T(1,128)} %param.11) | copy-start | bytes 1540
  0.7 21.2 %copy-start = (bf16[128,128,128]{2,1,0:T(8,128)(2,1)S(1)}, bf16[128,128,128]{2,1,0:T(8,128)(2,1)}, u32[]{:S(2)}) copy-start(bf16[128,128,128]{2,1,0:T(8,128)(2,1)} %weights_ref.1) | copy-start | bytes 12582916
  1.6 2.4 %copy-start.1 = (bf16[16,64,2048]{2,1,0:T(8,128)(2,1)S(1)}, bf16[16,64,2048]{2,1,0:T(8,128)(2,1)}, u32[]{:S(2)}) copy-start(bf16[16,64,2048]{2,1,0:T(8,128)(2,1)} %leg_ref.1) | copy-start | bytes 12582916
  4.1 1.4 %copy-start.2 = (bf16[6,64,2048]{2,1,0:T(8,128)(2,1)S(1)}, bf16[6,64,2048]{2,1,0:T(8,128)(2,1)}, u32[]{:S(2)}) copy-start(bf16[6,64,2048]{2,1,0:T(8,128)(2,1)} %alm_ref.1) | copy-start | bytes 4718596
  5.5 0.7 %copy-start.3 = (s32[4]{0:T(128)S(1)}, s32[4]{0:T(128)}, u32[]{:S(2)}) copy-start(s32[4]{0:T(128)} %cycle_ref.1) | copy-start | bytes 52

commit v2 on v1

--- a/solution.py
+++ b/solution.py
@@ -27,6 +27,10 @@
     return x + x * y * tail
 
 
+def loop(first, last, step):
+    return lax.fori_loop(first, last, step, 0, unroll=True if last <= 16 else 1)
+
+
 def exchange(bands, ords, cyc, npix, cycle_ref, order_ref, alm_ref, leg_ref, out_ref,
              alm_buf, leg_buf, part, landed, mine, gathered,
              alm_sem, leg_sem, rs_send, rs_recv, ag_send, ag_recv):
@@ -58,7 +62,7 @@
                             device_id_type=MESH)
         return 0
 
-    lax.fori_loop(1, devices, greet, 0)
+    loop(1, devices, greet)
 
     near = lax.broadcasted_iota(jnp.int32, (1, SUB, BLK), 1)
     far = lax.broadcasted_iota(jnp.int32, (1, SUB, BLK), 2) % SUB
@@ -105,9 +109,9 @@
             return 0
         return step
 
-    lax.fori_loop(1, bands, begin(scatter), 0)
-
-    m = order_ref[...]
+    loop(1, bands, begin(scatter))
+
+    m = jnp.concatenate([order_ref[...], order_ref[...]], axis=1)
     row = lax.broadcasted_iota(jnp.int32, (rows, BLK), 0)
     side = lax.broadcasted_iota(jnp.int32, (rows, BLK), 1) // half
     parity = jnp.zeros((rows, BLK), jnp.int32)
@@ -118,7 +122,7 @@
     sin_a = cosine(angle + jnp.where(side == 0, npix // 2, npix // 2 * 3), 2 * npix)
     factor = jnp.where(m == 0, 1.0, 2.0)
 
-    lax.fori_loop(1, bands, ended(scatter), 0)
+    loop(1, bands, ended(scatter))
 
     total = lax.fori_loop(1, bands, lambda t, acc: acc + landed[t], part[b])
     turned = factor * (total * cos_a + pltpu.roll(total, half, 1) * sin_a)
@@ -131,20 +135,20 @@
             src_ref=mine, dst_ref=gathered.at[t], send_sem=ag_send.at[t], recv_sem=ag_recv.at[t],
             device_id={"band": to // ords, "ord": lax.rem(to, ords)}, device_id_type=MESH)
 
-    lax.fori_loop(1, devices, begin(spread), 0)
+    loop(1, devices, begin(spread))
     out_ref[me] = turned
-    lax.fori_loop(1, devices, ended(spread), 0)
+    loop(1, devices, ended(spread))
 
     def place(t, _):
         out_ref[lax.rem(me - t + devices, devices)] = gathered[t]
         return 0
 
-    lax.fori_loop(1, devices, place, 0)
-
-
-def lens(bands, ords, cyc, npix, where_ref, band_ref, block_ref, coef_ref, weights_ref, sky_ref, lensed_ref,
+    loop(1, devices, place)
+
+
+def lens(bands, ords, cyc, npix, band_ref, block_ref, coef_ref, weights_ref, sky_ref, lensed_ref,
          high, low, table, picked, weights_buf, sem):
-    b, o = where_ref[0], where_ref[1]
+    b, o = lax.axis_index("band"), lax.axis_index("ord")
     here = npix // ords
     groups = here // WIDE
     depth = ords * BLK
@@ -207,8 +211,9 @@
                 at = g * WIDE + h * BLK
                 sky_ref[f, :, at:at + BLK] = value.astype(jnp.bfloat16)
 
-    for c in range(CHUNKS):
-        fetch(c).wait()
+    many = BLK // (4 * cyc)
+    groups_out = per_cycle // many
+    picked[...] = jnp.zeros(picked.shape, jnp.float32)
 
     def pick(p, _):
         for r in range(cyc):
@@ -217,22 +222,39 @@
             cycle, spot = block // per_cycle, block % per_cycle
             line = (spot // halves) * lines + band_ref[n] * (3 * cyc) + cycle
             for f in range(3):
-                picked[n, pl.ds(f, 1), :] = table[spot % halves, pl.ds(line + f * cyc, 1), :]
+                at = f * (many * cyc) + (p % many) * cyc + r
+                picked[p // many, pl.ds(at, 1), :] = table[spot % halves, pl.ds(line + f * cyc, 1), :]
         return 0
 
-    lax.fori_loop(0, per_cycle, pick, 0, unroll=2)
-
-    def apply(p, _):
-        for r in range(cyc):
-            n = r * per_cycle + p
-            made = lax.dot_general(
-                picked[n].astype(jnp.bfloat16), weights_buf[n], (((1,), (1,)), ((), ())),
-                preferred_element_type=jnp.float32)
+    lax.fori_loop(0, per_cycle, pick, 0, unroll=4)
+
+    for c in range(CHUNKS):
+        fetch(c).wait()
+
+    odd = lax.broadcasted_iota(jnp.int32, (BLK, BLK), 0) % 2
+    spot_of = lax.broadcasted_iota(jnp.int32, (BLK, BLK), 1) % (many * cyc) // 2
+
+    def apply(k, _):
+        source = picked[k]
+        right = jnp.concatenate(
+            [jnp.where(odd == 0, source, 0.0), jnp.where(odd == 1, source, 0.0)], axis=1).astype(jnp.bfloat16)
+        made = jnp.zeros((BLK, BLK), jnp.float32)
+        for p in range(many):
+            for r in range(0, cyc, 2):
+                n = r * per_cycle + k * many + p
+                left = jnp.concatenate([weights_buf[n], weights_buf[n + per_cycle]], axis=1)
+                product = lax.dot_general(
+                    left, right, (((1,), (1,)), ((), ())), preferred_element_type=jnp.float32)
+                made = jnp.where(spot_of == (p * cyc + r) // 2, product, made)
+        made = made.T
+        for p in range(many):
             for f in range(3):
-                lensed_ref[f, r:r + 1, pl.ds(pl.multiple_of(p * BLK, BLK), BLK)] = made[f:f + 1]
+                at = f * (many * cyc) + p * cyc
+                lanes_at = pl.ds(pl.multiple_of((k * many + p) * BLK, BLK), BLK)
+                lensed_ref[f, :, lanes_at] = made[at:at + cyc]
         return 0
 
-    lax.fori_loop(0, per_cycle, apply, 0, unroll=4)
+    lax.fori_loop(0, groups_out, apply, 0, unroll=2)
 
 
 def local(bands, ords, npix, alm, legendre, order_ids, cycle_number, src_band, src_block, weights):
@@ -247,7 +269,6 @@
     vmem = pl.BlockSpec(memory_space=pltpu.VMEM)
     smem = pl.BlockSpec(memory_space=pltpu.SMEM)
     anywhere = pl.BlockSpec(memory_space=pl.ANY)
-    doubled = jnp.concatenate([order_ids, order_ids]).reshape(1, 2 * orders)
     coef = pl.pallas_call(
         functools.partial(exchange, bands, ords, cyc, npix),
         out_shape=jax.ShapeDtypeStruct((devices, rows, BLK), jnp.float32),
@@ -268,10 +289,9 @@
             pltpu.SemaphoreType.DMA((devices,)),
         ],
         compiler_params=pltpu.CompilerParams(
-            collective_id=0, has_side_effects=True, vmem_limit_bytes=24 * 2**20),
+            collective_id=0, has_side_effects=True, vmem_limit_bytes=60 * 2**20),
         name="exchange",
-    )(cycle_number, doubled, alm, legendre)
-    place = jnp.stack([lax.axis_index("band"), lax.axis_index("ord")]).astype(jnp.int32)
+    )(cycle_number, order_ids.reshape(1, orders), alm, legendre)
     lines = bands * 3 * cyc * (here // WIDE)
     count = weights.shape[0]
     return pl.pallas_call(
@@ -280,19 +300,19 @@
             jax.ShapeDtypeStruct((3, cyc, here), jnp.bfloat16),
             jax.ShapeDtypeStruct((3, cyc, here), jnp.float32),
         ),
-        in_specs=[smem, smem, smem, vmem, anywhere],
+        in_specs=[smem, smem, vmem, anywhere],
         out_specs=(vmem, vmem),
         scratch_shapes=[
             pltpu.VMEM((lines, ords * BLK), jnp.float32),
             pltpu.VMEM((lines, ords * BLK), jnp.float32),
             pltpu.VMEM((WIDE // BLK, lines, BLK), jnp.float32),
-            pltpu.VMEM((count, 8, BLK), jnp.float32),
+            pltpu.VMEM((count * 4 // BLK, BLK, BLK), jnp.float32),
             pltpu.VMEM(weights.shape, jnp.bfloat16),
             pltpu.SemaphoreType.DMA((CHUNKS,)),
         ],
-        compiler_params=pltpu.CompilerParams(vmem_limit_bytes=48 * 2**20),
+        compiler_params=pltpu.CompilerParams(vmem_limit_bytes=60 * 2**20),
         name="lens",
-    )(place, src_band.reshape(count), src_block, coef, weights)
+    )(src_band.reshape(count), src_block, coef, weights)
 
 
 def solution(mesh):

time: 30.1 us -> 24.4 us (0.81)
  local copies, waits for them, and re-layouts: 4.52 us -> 0 us
  other arithmetic: 0.97 us -> 0 us
    unnamed x12 -> x0, local copies, waits for them, and re-layouts: 4.52 us -> none
    pallas_call x1, Pallas kernels: 8.09 us -> 6.82 us  [local(): pl.pallas_call(functools.partial(lens, bands, ords, cyc, npix), out_shape...]
    pallas_call x1, Pallas kernels: 15.7 us -> 16.8 us  [local(): pl.pallas_call(functools.partial(exchange, bands, ords, cyc, npix), out_s...]
    reshape x1 -> x0, other arithmetic: 0.9 us -> none  [local(): doubled = jnp.concatenate([order_ids, order_ids]).reshape(1, 2 * orders)]
where the time goes in v2:
time: 24.4 us; the launch traced here: 24.3 us
  Pallas kernels  23.6 us (97%)
  between operations  0.64 us (3%)
    pallas_call x1, Pallas kernels, local(): pl.pallas_call(functools.partial(exchange, bands, ords, cyc, npix), out_s...  16.8 us
    pallas_call x1, Pallas kernels, local(): pl.pallas_call(functools.partial(lens, bands, ords, cyc, npix), out_shape...  6.82 us

profile of v2, /device:TPU:0, one launch (start us, length us, event | category | flops | bytes accessed | tf_op | source)
XLA Modules:
  0.0 24.3 jit_solution(5113813962318863686)
XLA Ops:
  0.6 16.8 %exchange.1.coef_ref = f32[16,16,128]{2,1,0:T(8,128)} custom-call(s32[4]{0:T(128)} %cycle_ref.1, s32[1,64]{1,0:T(1,128)} %bitcast.2, bf16[6,64,2048]{2,1,0:T(8,128)(2,1)} %alm_ref.1, bf16[16,64,2048]{2,1,0:T(8,128)(2,1)} %leg_ref.1), custom_call_target="tpu_custom_call" | custom-call | tf_op jit(solution)/shard_map/exchange/pallas_call | solution.py:272
  17.5 6.8 %lens.1 = (bf16[3,4,4096]{2,1,0:T(4,128)(2,1)}, f32[3,4,4096]{2,1,0:T(4,128)}) custom-call(s32[128]{0:T(128)} %bitcast.3, s32[128]{0:T(128)} %block_ref.1, f32[16,16,128]{2,1,0:T(8,128)} %exchange.1.coef_ref, bf16[128,128,128]{2,1,0:T(8,128)(2,1)} %weights_ref.1), custom_call_target="tpu_custom_call" | custom-call | tf_op jit(solution)/shard_map/lens/pallas_call | solution.py:297

commit v3 on v2

--- a/solution.py
+++ b/solution.py
@@ -226,7 +226,7 @@
                 picked[p // many, pl.ds(at, 1), :] = table[spot % halves, pl.ds(line + f * cyc, 1), :]
         return 0
 
-    lax.fori_loop(0, per_cycle, pick, 0, unroll=4)
+    lax.fori_loop(0, per_cycle, pick, 0, unroll=2)
 
     for c in range(CHUNKS):
         fetch(c).wait()
@@ -254,7 +254,7 @@
                 lensed_ref[f, :, lanes_at] = made[at:at + cyc]
         return 0
 
-    lax.fori_loop(0, groups_out, apply, 0, unroll=2)
+    lax.fori_loop(0, groups_out, apply, 0)
 
 
 def local(bands, ords, npix, alm, legendre, order_ids, cycle_number, src_band, src_block, weights):

time: 24.4 us -> 24.8 us (1.016)
  Pallas kernels: 23.6 us -> 24 us
    pallas_call x1, Pallas kernels: 6.82 us -> 7.21 us  [local(): pl.pallas_call(functools.partial(lens, bands, ords, cyc, npix), out_shape...]
where the time goes in v3:
time: 24.8 us; the launch traced here: 24.7 us
  Pallas kernels  24 us (97%)
  between operations  0.64 us (3%)
    pallas_call x1, Pallas kernels, local(): pl.pallas_call(functools.partial(exchange, bands, ords, cyc, npix), out_s...  16.8 us
    pallas_call x1, Pallas kernels, local(): pl.pallas_call(functools.partial(lens, bands, ords, cyc, npix), out_shape...  7.21 us

profile of v3, /device:TPU:0, one launch (start us, length us, event | category | flops | bytes accessed | tf_op | source)
XLA Modules:
  0.0 24.7 jit_solution(3636029279866180285)
XLA Ops:
  0.6 16.8 %exchange.1.coef_ref = f32[16,16,128]{2,1,0:T(8,128)} custom-call(s32[4]{0:T(128)} %cycle_ref.1, s32[1,64]{1,0:T(1,128)} %bitcast.2, bf16[6,64,2048]{2,1,0:T(8,128)(2,1)} %alm_ref.1, bf16[16,64,2048]{2,1,0:T(8,128)(2,1)} %leg_ref.1), custom_call_target="tpu_custom_call" | custom-call | tf_op jit(solution)/shard_map/exchange/pallas_call | solution.py:272
  17.5 7.2 %lens.1 = (bf16[3,4,4096]{2,1,0:T(4,128)(2,1)}, f32[3,4,4096]{2,1,0:T(4,128)}) custom-call(s32[128]{0:T(128)} %bitcast.3, s32[128]{0:T(128)} %block_ref.1, f32[16,16,128]{2,1,0:T(8,128)} %exchange.1.coef_ref, bf16[128,128,128]{2,1,0:T(8,128)(2,1)} %weights_ref.1), custom_call_target="tpu_custom_call" | custom-call | tf_op jit(solution)/shard_map/lens/pallas_call | solution.py:297
